TPU v7x, 256 devices: a whole 4x4x8 slice. The times are simulated.
256 devices in a mesh: dp: 256 (over x, y, z, core).
Axes of the slice: x: 4, y: 4, z: 8, core: 2. Of those that a mesh axis runs over, the one named last changes fastest.
Arguments:
- image_embed: bfloat16 [131072, 1152], P('dp'), may hold values from -0.1796875 to 0.1796875
- text_embed: bfloat16 [131072, 1152], P('dp'), may hold values from -0.1796875 to 0.1796875
- logit_scale: float32 [1], replicated, may hold values from 4 to 16
- logit_bias: float32 [1], replicated, may hold values from -3 to -1
Outputs:
- row_loss: float32 [131072], P('dp')
- image_grad: float32 [131072, 1152], P('dp')
- text_grad: float32 [131072, 1152], P('dp')
All inputs are finite; a program needn't handle non-finite values.
Results may differ from a plain program's by a relative error of at most 0.0046.
Values may be sent and summed in bfloat16 or wider, within the bound.
A program may use at most 64 MiB of HBM per device.

v0:
```python
import jax
import jax.numpy as jnp
from jax import lax
from jax.sharding import PartitionSpec as P

REACH = 2
WINDOW = 5


eps_norm = 1e-06


def shifted(block, axis, distance):
    devices = range(lax.axis_size(axis))
    route = [((i - distance) % len(devices), i) for i in devices]
    return lax.ppermute(block, axis, route)


def unit_rows(raw_rows):
    values = raw_rows.astype(jnp.float32)
    length = jnp.sqrt(jnp.sum(values * values, axis=1, keepdims=True) + eps_norm)
    return (values / length, length)


def unit_grad(grad_unit, unit_values, length):
    along_unit = jnp.sum(grad_unit * unit_values, axis=1, keepdims=True)
    return (grad_unit - unit_values * along_unit) / length


def pair_block(image_rows, text_rows, scale_value, bias_value, positive):
    cosine = lax.dot_general(
        image_rows, text_rows, (((1,), (1,)), ((), ())), preferred_element_type=jnp.float32
    )
    logits = scale_value * cosine + bias_value
    if positive:
        target = jnp.eye(logits.shape[0], dtype=logits.dtype)
    else:
        target = jnp.zeros_like(logits)
    pair_loss = jax.nn.softplus(logits) - target * logits
    weights = (scale_value * (jax.nn.sigmoid(logits) - target)).astype(jnp.bfloat16)
    return (jnp.sum(pair_loss, axis=1), weights)


def text_partial(weights, image_rows):
    return lax.dot_general(
        weights, image_rows, (((0,), (0,)), ((), ())), preferred_element_type=jnp.float32
    )


def fetch(payload):
    from_lower = []
    from_upper = []
    moving_up = payload
    moving_down = payload
    for distance in range(REACH):
        moving_up = shifted(moving_up, "dp", 1)
        moving_down = shifted(moving_down, "dp", -1)
        from_lower.append(moving_up)
        from_upper.append(moving_down)
    return (from_lower, from_upper)


def local(image_embed, text_embed, logit_scale, logit_bias):
    scale_value = logit_scale[0]
    bias_value = logit_bias[0]
    image_unit, image_length = unit_rows(image_embed)
    text_unit, text_length = unit_rows(text_embed)
    image_rows = image_unit.astype(jnp.bfloat16)
    text_rows = text_unit.astype(jnp.bfloat16)
    own_rows = image_rows.shape[0]
    payload = text_rows[None]
    from_lower, from_upper = fetch(payload)
    loss_total, weights = pair_block(image_rows, text_rows, scale_value, bias_value, True)
    image_total = jnp.dot(weights, text_rows, preferred_element_type=jnp.float32)
    text_total = text_partial(weights, image_rows)
    lower_parts = []
    upper_parts = []
    for position, received in enumerate(from_lower + from_upper):
        row_sum, weights = pair_block(image_rows, received[0], scale_value, bias_value, False)
        loss_total = loss_total + row_sum
        image_total = image_total + jnp.dot(
            weights, received[0], preferred_element_type=jnp.float32
        )
        if position < REACH:
            lower_parts.append(text_partial(weights, image_rows))
        else:
            upper_parts.append(text_partial(weights, image_rows))
    for distance in range(REACH):
        text_total = text_total + shifted(lower_parts[distance], "dp", -(distance + 1))
        text_total = text_total + shifted(upper_parts[distance], "dp", distance + 1)
    row_loss = loss_total / (WINDOW * own_rows)
    image_grad = unit_grad(image_total, image_unit, image_length)
    text_grad = unit_grad(text_total, text_unit, text_length)
    return (row_loss, image_grad, text_grad)


def solution(mesh):
    return jax.shard_map(
        local,
        mesh=mesh,
        in_specs=(P("dp", None), P("dp", None), P(), P()),
        out_specs=(P("dp"), P("dp", None), P("dp", None)),
        check_vma=False,
    )
```

profile of v0, /device:TPU:0, one launch (start us, length us, event | category | flops | bytes accessed | tf_op | source)
XLA Modules:
  0.0 145.0 jit_solution(2757187757911384552)
XLA Ops:
  0.6 0.0 copy-start
  0.6 1.7 %fusion.5 = f32[512]{0:T(512)S(1)} fusion(bf16[512,1152]{1,0:T(8,128)(2,1)} %param.5), kind=kLoop, calls=%fused_computation.18 | loop fusion | flops 1768960 | bytes 1181696 | tf_op jit(solution)/shard_map/reduce_sum | solution.py:21
  2.3 1.6 %convert_bitcast_fusion = bf16[1,512,1152]{2,1,0:T(8,128)(2,1)S(1)} fusion(f32[512]{0:T(512)S(1)} %add_sqrt_fusion, bf16[512,1152]{1,0:T(8,128)(2,1)} %param.5), kind=kLoop, calls=%fused_computation.63 | loop fusion | flops 1769472 | bytes 2361344 | tf_op jit(solution)/shard_map/broadcast_in_dim | solution.py:71
  4.0 0.0 copy-start.1
  4.0 8.3 %collective-permute-start.2 = (bf16[1,512,1152]{2,1,0:T(8,128)(2,1)S(1)}, bf16[1,512,1152]{2,1,0:T(8,128)(2,1)S(1)}, u32[]{:S(2)}, u32[]{:S(2)}) collective-permute-start(bf16[1,512,1152]{2,1,0:T(8,128)(2,1)S(1)} %convert_bitcast_fusion), channel_id=1, source_target_pairs={{1,0},{2,1},{3,2},{4,3},{5,4},{6,5},{7,6},{8,7},{9,8},{10,9},{11,1... | collective-permute-start | bytes 3538952 | tf_op jit(solution)/shard_map/ppermute | solution.py:16
  12.2 0.0 collective-permute-start
  12.3 0.0 copy-done
  12.3 0.3 fusion.4
  12.6 0.4 fusion.33
  14.3 0.0 copy-done.1
  14.3 1.5 %fusion.21 = (f32[512]{0:T(512)S(1)}, f32[512,512]{0,1:T(8,128)S(1)}) fusion(f32[]{:T(128)} %bitcast.59, bf16[512,1152]{1,0:T(8,128)(2,1)S(1)} %fusion.33, f32[512]{0:T(512)S(1)} %add_sqrt_fusion, bf16[512,1152]{1,0:T(8,128)(2,1)S(1)} %copy-done.1, f32[]{:T(128)} %bitcast.44), kind=kOutput, calls=%fused_computation.43 | convolution fusion | flops 608894464 | bytes 3411976 | tf_op jit(solution)/shard_map/dot_general | solution.py:31
  15.7 1.1 fusion.30
  16.8 9.2 %collective-permute-done.2 = bf16[1,512,1152]{2,1,0:T(8,128)(2,1)S(1)} collective-permute-done((bf16[1,512,1152]{2,1,0:T(8,128)(2,1)S(1)}, bf16[1,512,1152]{2,1,0:T(8,128)(2,1)S(1)}, u32[]{:S(2)}, u32[]{:S(2)}) %collective-permute-start.2) | collective-permute-done | bytes 1179680 | tf_op jit(solution)/shard_map/ppermute | solution.py:16
  26.0 1.5 %fusion.27 = (f32[512]{0:T(512)S(1)}, f32[512,512]{0,1:T(8,128)S(1)}) fusion(f32[]{:T(128)} %bitcast.61, bf16[512,1152]{1,0:T(8,128)(2,1)S(1)} %fusion.33, bf16[1,512,1152]{2,1,0:T(8,128)(2,1)S(1)} %collective-permute-done.2, f32[]{:T(128)} %bitcast.51), kind=kOutput, calls=%fused_computation.49 | convolution fusion | flops 606862848 | bytes 3409928 | tf_op jit(solution)/shard_map/dot_general | solution.py:31
  27.4 1.0 fusion.36
  28.4 0.1 collective-permute-start.5
  28.5 7.4 %collective-permute-start.3 = (bf16[1,512,1152]{2,1,0:T(8,128)(2,1)S(1)}, bf16[1,512,1152]{2,1,0:T(8,128)(2,1)S(1)}, u32[]{:S(2)}, u32[]{:S(2)}) collective-permute-start(bf16[1,512,1152]{2,1,0:T(8,128)(2,1)S(1)} %collective-permute-done.2), channel_id=1, source_target_pairs={{1,0},{2,1},{3,2},{4,3},{5,4},{6,5},{7,6},{8,7},{9,8},{10,9},{11,1... | collective-permute-start | bytes 3538952 | tf_op jit(solution)/shard_map/ppermute | solution.py:16
  35.9 0.0 collective-permute-done
  35.9 1.5 %fusion.23 = (f32[512]{0:T(512)S(1)}, f32[512,512]{0,1:T(8,128)S(1)}) fusion(f32[]{:T(128)} %bitcast.63, bf16[512,1152]{1,0:T(8,128)(2,1)S(1)} %fusion.33, bf16[1,512,1152]{2,1,0:T(8,128)(2,1)S(1)} %collective-permute-done, f32[]{:T(128)} %bitcast.53), kind=kOutput, calls=%fused_computation.45 | convolution fusion | flops 606862848 | bytes 3409928 | tf_op jit(solution)/shard_map/dot_general | solution.py:31
  37.4 1.0 fusion.34
  38.4 0.5 collective-permute-start.4
  38.9 0.1 collective-permute-start.1
  39.0 0.9 fusion.13
  39.9 0.9 convolution_add_fusion.3
  40.8 8.8 %collective-permute-done.3 = bf16[1,512,1152]{2,1,0:T(8,128)(2,1)S(1)} collective-permute-done((bf16[1,512,1152]{2,1,0:T(8,128)(2,1)S(1)}, bf16[1,512,1152]{2,1,0:T(8,128)(2,1)S(1)}, u32[]{:S(2)}, u32[]{:S(2)}) %collective-permute-start.3) | collective-permute-done | bytes 1179680 | tf_op jit(solution)/shard_map/ppermute | solution.py:16
  49.6 1.5 %fusion.29 = (f32[512]{0:T(512)S(1)}, f32[512,512]{0,1:T(8,128)S(1)}) fusion(f32[]{:T(128)} %bitcast.60, bf16[512,1152]{1,0:T(8,128)(2,1)S(1)} %fusion.33, bf16[1,512,1152]{2,1,0:T(8,128)(2,1)S(1)} %collective-permute-done.3, f32[]{:T(128)} %bitcast.50), kind=kOutput, calls=%fused_computation.51 | convolution fusion | flops 606862848 | bytes 3409928 | tf_op jit(solution)/shard_map/dot_general | solution.py:31
  51.1 1.0 fusion.37
  52.1 0.1 collective-permute-start.7
  52.2 36.6 %collective-permute-done.1 = bf16[1,512,1152]{2,1,0:T(8,128)(2,1)S(1)} collective-permute-done((bf16[1,512,1152]{2,1,0:T(8,128)(2,1)S(1)}, bf16[1,512,1152]{2,1,0:T(8,128)(2,1)S(1)}, u32[]{:S(2)}, u32[]{:S(2)}) %collective-permute-start.1) | collective-permute-done | bytes 1179680 | tf_op jit(solution)/shard_map/ppermute | solution.py:16
  88.8 1.5 %fusion.25 = (f32[512]{0:T(512)S(1)}, f32[512,512]{0,1:T(8,128)S(1)}) fusion(f32[]{:T(128)} %bitcast.62, bf16[512,1152]{1,0:T(8,128)(2,1)S(1)} %fusion.33, bf16[1,512,1152]{2,1,0:T(8,128)(2,1)S(1)} %collective-permute-done.1, f32[]{:T(128)} %bitcast.52), kind=kOutput, calls=%fused_computation.47 | convolution fusion | flops 606862848 | bytes 3409928 | tf_op jit(solution)/shard_map/dot_general | solution.py:31
  90.2 1.0 fusion.35
  91.2 0.1 collective-permute-start.6
  91.3 0.6 add_multiply_fusion
  91.9 1.0 fusion
  92.9 1.2 multiply_reduce_fusion.1
  94.1 1.9 %subtract_divide_fusion.1 = f32[512,1152]{1,0:T(8,128)} fusion(f32[512,1152]{1,0:T(8,128)S(1)} %get-tuple-element.14, f32[512]{0:T(512)S(1)} %get-tuple-element.13, f32[512]{0:T(512)S(1)} %add_sqrt_fusion.1, bf16[512,1152]{1,0:T(8,128)(2,1)S(1)} %copy-done), kind=kLoop, calls=%fused_computation.21 | loop fusion | flops 2949120 | bytes 5902336 | tf_op jit(solution)/shard_map/div | solution.py:27
  96.0 0.0 collective-permute-done.5
  96.0 0.0 collective-permute-done.4
  96.0 15.8 %collective-permute-done.7 = f32[512,1152]{1,0:T(8,128)S(1)} collective-permute-done((f32[512,1152]{1,0:T(8,128)S(1)}, f32[512,1152]{1,0:T(8,128)S(1)}, u32[]{:S(2)}, u32[]{:S(2)}) %collective-permute-start.7) | collective-permute-done | bytes 2359328 | tf_op jit(solution)/shard_map/ppermute | solution.py:16
  111.8 29.8 %collective-permute-done.6 = f32[512,1152]{1,0:T(8,128)S(1)} collective-permute-done((f32[512,1152]{1,0:T(8,128)S(1)}, f32[512,1152]{1,0:T(8,128)S(1)}, u32[]{:S(2)}, u32[]{:S(2)}) %collective-permute-start.6) | collective-permute-done | bytes 2359328 | tf_op jit(solution)/shard_map/ppermute | solution.py:16
  141.6 1.5 %multiply_reduce_fusion = (f32[512]{0:T(512)S(1)}, f32[512,1152]{1,0:T(8,128)S(1)}) fusion(f32[512]{0:T(512)S(1)} %add_sqrt_fusion, bf16[512,1152]{1,0:T(8,128)(2,1)S(1)} %copy-done.1, f32[512,1152]{1,0:T(8,128)S(1)} %collective-permute-done.7, f32[512,1152]{1,0:T(8,128)S(1)} %collective-permute-done.6, f32[512,1152]{1,0:T(8,128)S(1)} %collective-permute-done.5, ...), kind=kOutput, calls=%fused_computation.20 | convolution fusion | flops 610795008 | bytes 15208452 | tf_op jit(solution)/shard_map/dot_general | solution.py:45
  143.1 1.9 %subtract_divide_fusion = f32[512,1152]{1,0:T(8,128)} fusion(f32[512,1152]{1,0:T(8,128)S(1)} %get-tuple-element.16, f32[512]{0:T(512)S(1)} %get-tuple-element.15, f32[512]{0:T(512)S(1)} %add_sqrt_fusion, bf16[512,1152]{1,0:T(8,128)(2,1)S(1)} %copy-done.1), kind=kLoop, calls=%fused_computation.19 | loop fusion | flops 2949120 | bytes 5902336 | tf_op jit(solution)/shard_map/div | solution.py:27
  (2 shorter events, 0.0 us)
Async XLA Ops:
  0.6 11.6 %copy-start = (bf16[512,1152]{1,0:T(8,128)(2,1)S(1)}, bf16[512,1152]{1,0:T(8,128)(2,1)}, u32[]{:S(2)}) copy-start(bf16[512,1152]{1,0:T(8,128)(2,1)} %param.4) | copy-start | bytes 3538948
  4.0 10.3 %copy-start.1 = (bf16[512,1152]{1,0:T(8,128)(2,1)S(1)}, bf16[512,1152]{1,0:T(8,128)(2,1)}, u32[]{:S(2)}) copy-start(bf16[512,1152]{1,0:T(8,128)(2,1)} %param.5) | copy-start | bytes 3538948
  4.0 22.0 %collective-permute-start.2 = (bf16[1,512,1152]{2,1,0:T(8,128)(2,1)S(1)}, bf16[1,512,1152]{2,1,0:T(8,128)(2,1)S(1)}, u32[]{:S(2)}, u32[]{:S(2)}) collective-permute-start(bf16[1,512,1152]{2,1,0:T(8,128)(2,1)S(1)} %convert_bitcast_fusion), channel_id=1, source_target_pairs={{1,0},{2,1},{3,2},{4,3},{5,4},{6,5},{7,6},{8,7},{9,8},{10,9},{11,1... | collective-permute-start | bytes 3538952 | tf_op jit(solution)/shard_map/ppermute | solution.py:16
  12.2 23.7 %collective-permute-start = (bf16[1,512,1152]{2,1,0:T(8,128)(2,1)S(1)}, bf16[1,512,1152]{2,1,0:T(8,128)(2,1)S(1)}, u32[]{:S(2)}, u32[]{:S(2)}) collective-permute-start(bf16[1,512,1152]{2,1,0:T(8,128)(2,1)S(1)} %convert_bitcast_fusion), channel_id=1, source_target_pairs={{255,0},{0,1},{1,2},{2,3},{3,4},{4,5},{5,6},{6,7},{7,8},{8,9},{9,1... | collective-permute-start | bytes 3538952 | tf_op jit(solution)/shard_map/ppermute | solution.py:16
  28.4 67.5 %collective-permute-start.5 = (f32[512,1152]{1,0:T(8,128)S(1)}, f32[512,1152]{1,0:T(8,128)S(1)}, u32[]{:S(2)}, u32[]{:S(2)}) collective-permute-start(f32[512,1152]{1,0:T(8,128)S(1)} %fusion.36), channel_id=1, source_target_pairs={{255,0},{0,1},{1,2},{2,3},{3,4},{4,5},{5,6},{6,7},{7,8},{8,9},{9,1... | collective-permute-start | bytes 7077896 | tf_op jit(solution)/shard_map/ppermute | solution.py:16
  28.5 21.1 %collective-permute-start.3 = (bf16[1,512,1152]{2,1,0:T(8,128)(2,1)S(1)}, bf16[1,512,1152]{2,1,0:T(8,128)(2,1)S(1)}, u32[]{:S(2)}, u32[]{:S(2)}) collective-permute-start(bf16[1,512,1152]{2,1,0:T(8,128)(2,1)S(1)} %collective-permute-done.2), channel_id=1, source_target_pairs={{1,0},{2,1},{3,2},{4,3},{5,4},{6,5},{7,6},{8,7},{9,8},{10,9},{11,1... | collective-permute-start | bytes 3538952 | tf_op jit(solution)/shard_map/ppermute | solution.py:16
  38.4 57.6 %collective-permute-start.4 = (f32[512,1152]{1,0:T(8,128)S(1)}, f32[512,1152]{1,0:T(8,128)S(1)}, u32[]{:S(2)}, u32[]{:S(2)}) collective-permute-start(f32[512,1152]{1,0:T(8,128)S(1)} %fusion.34), channel_id=1, source_target_pairs={{1,0},{2,1},{3,2},{4,3},{5,4},{6,5},{7,6},{8,7},{9,8},{10,9},{11,1... | collective-permute-start | bytes 7077896 | tf_op jit(solution)/shard_map/ppermute | solution.py:16
  38.9 49.9 %collective-permute-start.1 = (bf16[1,512,1152]{2,1,0:T(8,128)(2,1)S(1)}, bf16[1,512,1152]{2,1,0:T(8,128)(2,1)S(1)}, u32[]{:S(2)}, u32[]{:S(2)}) collective-permute-start(bf16[1,512,1152]{2,1,0:T(8,128)(2,1)S(1)} %collective-permute-done), channel_id=1, source_target_pairs={{255,0},{0,1},{1,2},{2,3},{3,4},{4,5},{5,6},{6,7},{7,8},{8,9},{9,1... | collective-permute-start | bytes 3538952 | tf_op jit(solution)/shard_map/ppermute | solution.py:16
  52.1 59.7 %collective-permute-start.7 = (f32[512,1152]{1,0:T(8,128)S(1)}, f32[512,1152]{1,0:T(8,128)S(1)}, u32[]{:S(2)}, u32[]{:S(2)}) collective-permute-start(f32[512,1152]{1,0:T(8,128)S(1)} %fusion.37), channel_id=1, source_target_pairs={{254,0},{255,1},{0,2},{1,3},{2,4},{3,5},{4,6},{5,7},{6,8},{7,9},{8... | collective-permute-start | bytes 7077896 | tf_op jit(solution)/shard_map/ppermute | solution.py:16
  91.2 50.4 %collective-permute-start.6 = (f32[512,1152]{1,0:T(8,128)S(1)}, f32[512,1152]{1,0:T(8,128)S(1)}, u32[]{:S(2)}, u32[]{:S(2)}) collective-permute-start(f32[512,1152]{1,0:T(8,128)S(1)} %fusion.35), channel_id=1, source_target_pairs={{2,0},{3,1},{4,2},{5,3},{6,4},{7,5},{8,6},{9,7},{10,8},{11,9},{12,... | collective-permute-start | bytes 7077896 | tf_op jit(solution)/shard_map/ppermute | solution.py:16
where the time goes:
time: 147 us; the launch traced here: 145 us
  waiting for transfers between devices  100 us (68%)
  matrix products  17.8 us (12%)
  starting transfers between devices  16.5 us (11%)
  other arithmetic  8.36 us (6%)
  between operations  2.07 us (1%)
    ppermute x8, waiting for transfers between devices, shifted(): return lax.ppermute(block, axis, route)  100 us
    ppermute x8, starting transfers between devices, shifted(): return lax.ppermute(block, axis, route)  16.5 us
    dot_general x5, matrix products, pair_block(): lax.dot_general(image_rows, text_rows, (((1,), (1,)), ((), ())), preferre...  7.34 us
    dot_general x5, matrix products, text_partial(): lax.dot_general(weights, image_rows, (((0,), (0,)), ((), ())), preferred_...  5.4 us
    dot_general x4, matrix products, local(): jnp.dot(weights, received[0], preferred_element_type=jnp.float32)  4.01 us
    div x2, other arithmetic, unit_grad(): return (grad_unit - unit_values * along_unit) / length  3.78 us
  transfers between devices with their start and end apart: 8, of which 5 were waited for; matrix products, arithmetic and copies ran while one was open for 13% of the time, Pallas kernels for 0%

commit v1 on v0

v1 whole, which is shorter than its diff:
```python
import functools

import jax
import jax.numpy as jnp
from jax import lax
from jax.experimental import pallas as pl
from jax.experimental.pallas import tpu as pltpu
from jax.sharding import PartitionSpec as P

MESH = pl.DeviceIdType.MESH
REACH = 2
WINDOW = 5
EPS = 1e-06
UP, DOWN, RELAY, SIBLING, OWN = range(5)
ROUNDS = 4


def inverse_length(rows):
    return lax.rsqrt(jnp.sum(rows * rows, axis=1, keepdims=True) + EPS)


def exchange(n, img, txt, scale_ref, bias_ref, image_grad, text_grad, loss_out,
             buf, own, chunk, total, inverse, loss_acc, load_sem, send_sem, recv_sem):
    rows = img.shape[0]
    part = rows // 2
    me = lax.axis_index("dp")
    core = lax.rem(me, 2)
    sibling = me + 1 - 2 * core
    upper = lax.rem(me + 2, n)
    lower = lax.rem(me + n - 2, n)
    relayed = 1 - core

    barrier = pltpu.get_barrier_semaphore()
    for other in (upper, lower, sibling):
        pl.semaphore_signal(barrier, inc=1, device_id=(other,), device_id_type=MESH)
    loads = [pltpu.make_async_copy(source, buf.at[OWN, kind], load_sem.at[kind]) for kind, source in enumerate((txt, img))]
    for load in loads:
        load.start()
    pl.semaphore_wait(barrier, 3)

    def place(step):
        return step // 2, pl.ds(pl.multiple_of(lax.rem(step, 2) * part, part), part)

    def outgoing(source, target, way, step):
        kind, span = step // 2, pl.ds((step % 2) * part, part)
        return pltpu.make_async_remote_copy(
            source[kind].at[span], buf.at[way, kind, span], send_sem.at[way, step], recv_sem.at[way, step],
            device_id=(target,), device_id_type=MESH,
        )

    def relay(step):
        kind, span = place(step)
        return pltpu.make_async_remote_copy(
            buf.at[relayed, kind, span], buf.at[RELAY, kind, span], send_sem.at[RELAY, step], recv_sem.at[RELAY, step],
            device_id=(sibling,), device_id_type=MESH,
        )

    def arrived(way, step):
        kind, span = place(step)
        return pltpu.make_async_remote_copy(
            buf.at[way, kind, span], buf.at[way, kind, span], send_sem.at[way, step], recv_sem.at[way, step],
            device_id=(sibling,), device_id_type=MESH,
        )

    sends = []
    for step in range(ROUNDS):
        for way, target in ((UP, upper), (DOWN, lower)):
            sends.append(outgoing((txt, img), target, way, step))
    for step in range(ROUNDS):
        sends.append(outgoing((txt, img), sibling, SIBLING, step))
    for send in sends:
        send.start()

    scale = scale_ref[0]
    bias = bias_ref[0]
    for load in loads:
        load.wait()
    total[...] = jnp.zeros_like(total)
    loss_acc[...] = jnp.zeros_like(loss_acc)

    @pl.loop(0, 2)
    def _(kind):
        @pl.loop(0, rows // 128)
        def _(tile):
            span = pl.ds(pl.multiple_of(tile * 128, 128), 128)
            values = buf[OWN, 1 - kind, span].astype(jnp.float32)
            factor = inverse_length(values)
            inverse[kind, span] = factor
            own[kind, span] = (values * factor).astype(jnp.bfloat16)

    def pairs(way, step, is_own):
        kind, span = place(step)

        for tile in range(part // 128):
            rows_here = pl.ds(pl.multiple_of(lax.rem(step, 2) * part + tile * 128, 128), 128)
            values = buf[way, kind, rows_here].astype(jnp.float32)
            chunk[tile * 128:(tile + 1) * 128] = (values * inverse_length(values)).astype(jnp.bfloat16)
        offset = jnp.where(is_own, lax.rem(step, 2) * part, -2 * rows)
        for tile in range(rows // 256):
            held = pl.ds(tile * 256, 256)
            cosine = lax.dot_general(own[kind, held], chunk[...], (((1,), (1,)), ((), ())), preferred_element_type=jnp.float32)
            logits = scale * cosine + bias
            row = lax.broadcasted_iota(jnp.int32, logits.shape, 0) + tile * 256
            column = lax.broadcasted_iota(jnp.int32, logits.shape, 1)
            positive = row - column == offset
            grown = jnp.exp(logits)
            above = 1.0 + grown
            small = grown * (1.0 - grown * (0.5 - grown * (1.0 / 3.0)))
            loss = jnp.where(grown < 0.0078125, small, jnp.log(above)) - jnp.where(positive, logits, 0.0)
            loss_acc[kind, held] += functools.reduce(jnp.add, [loss[:, i:i + 128] for i in range(0, part, 128)])
            weights = (scale * (grown * pl.reciprocal(above) - jnp.where(positive, 1.0, 0.0))).astype(jnp.bfloat16)
            total[kind, held] += jnp.dot(weights, chunk[...], preferred_element_type=jnp.float32)

    @pl.loop(0, ROUNDS)
    def _(step):
        pairs(OWN, step, True)

    @pl.loop(0, ROUNDS)
    def _(step):
        arrived(SIBLING, step).wait_recv()
        pairs(SIBLING, step, False)

    def finish(kind, out):
        @pl.loop(0, rows // 64)
        def _(tile):
            span = pl.ds(pl.multiple_of(tile * 64, 64), 64)
            factor = inverse[kind, span]
            unit = buf[OWN, 1 - kind, span].astype(jnp.float32) * factor
            summed = total[kind, span]
            along = jnp.sum(summed * unit, axis=1, keepdims=True)
            out[span] = (summed - unit * along) * factor

    @pl.loop(0, ROUNDS * 3)
    def _(turn):
        step, order = turn // 3, lax.rem(turn, 3)
        way = jnp.where(order == 0, relayed, jnp.where(order == 1, 1 - relayed, RELAY))
        arrived(way, step).wait_recv()

        @pl.when(order == 0)
        def _():
            relay(step).start()

        pairs(way, step, False)

        @pl.when(turn == 5)
        def _():
            finish(0, image_grad)

    finish(1, text_grad)
    ones = jnp.full((8, 128), 1.0, jnp.float32)
    row_loss = lax.dot_general(
        ones, loss_acc[0], (((1,), (1,)), ((), ())), preferred_element_type=jnp.float32, precision=lax.Precision.HIGHEST
    )
    loss_out[...] = row_loss * (1.0 / (WINDOW * rows))
    for send in sends:
        send.wait_send()
    for step in range(ROUNDS):
        relay(step).wait_send()


def local(n, image_embed, text_embed, logit_scale, logit_bias):
    rows, width = image_embed.shape
    image_grad, text_grad, loss = pl.pallas_call(
        functools.partial(exchange, n),
        out_shape=(
            pltpu.VMEM((rows, width), jnp.float32),
            pltpu.VMEM((rows, width), jnp.float32),
            pltpu.VMEM((8, rows), jnp.float32),
        ),
        in_specs=[
            pl.BlockSpec(memory_space=pl.ANY),
            pl.BlockSpec(memory_space=pl.ANY),
            pl.BlockSpec(memory_space=pltpu.SMEM),
            pl.BlockSpec(memory_space=pltpu.SMEM),
        ],
        out_specs=[pl.BlockSpec(memory_space=pltpu.VMEM)] * 3,
        scratch_shapes=[
            pltpu.VMEM((5, 2, rows, width), jnp.bfloat16),
            pltpu.VMEM((2, rows, width), jnp.bfloat16),
            pltpu.VMEM((rows // 2, width), jnp.bfloat16),
            pltpu.VMEM((2, rows, width), jnp.float32),
            pltpu.VMEM((2, rows, 1), jnp.float32),
            pltpu.VMEM((2, rows, 128), jnp.float32),
            pltpu.SemaphoreType.DMA((2,)),
            pltpu.SemaphoreType.DMA((4, ROUNDS)),
            pltpu.SemaphoreType.DMA((4, ROUNDS)),
        ],
        compiler_params=pltpu.CompilerParams(
            collective_id=0, has_side_effects=True, vmem_limit_bytes=48 * 1024 * 1024
        ),
    )(image_embed, text_embed, logit_scale, logit_bias)
    return loss[0], image_grad, text_grad


def solution(mesh):
    return jax.shard_map(
        functools.partial(local, mesh.shape["dp"]),
        mesh=mesh,
        in_specs=(P("dp", None), P("dp", None), P(), P()),
        out_specs=(P("dp"), P("dp", None), P("dp", None)),
        check_vma=False,
    )
```

time: 147 us -> 77.5 us (0.53)
  the two profiles are of different devices: /device:TPU:0 before, /device:TPU:1 now
where the time goes in v1:
time: 77.5 us; the launch traced here: 77.3 us
  Pallas kernels  70.7 us (91%)
  local copies, waits for them, and re-layouts  4.65 us (6%)
  between operations  1.94 us (3%)
    pallas_call x1, Pallas kernels, local(): pl.pallas_call(functools.partial(exchange, n), out_shape=(pltpu.VMEM((row...  70.7 us
    unnamed x4, local copies, waits for them, and re-layouts  4.07 us

profile of v1, /device:TPU:1, one launch (start us, length us, event | category | flops | bytes accessed | tf_op | source)
XLA Modules:
  0.0 77.3 jit_solution(9609761961783653003)
XLA Ops:
  1.9 0.0 copy-start
  1.9 1.3 %copy-done = bf16[512,1152]{1,0:T(8,128)(2,1)S(1)} copy-done((bf16[512,1152]{1,0:T(8,128)(2,1)S(1)}, bf16[512,1152]{1,0:T(8,128)(2,1)}, u32[]{:S(2)}) %copy-start) | copy-done | bytes 1179672
  3.2 70.7 %shard_map.67 = (f32[512,1152]{1,0:T(8,128)S(1)}, f32[512,1152]{1,0:T(8,128)S(1)}, f32[8,512]{1,0:T(8,128)S(1)}) custom-call(bf16[512,1152]{1,0:T(8,128)(2,1)S(1)} %copy-done, bf16[512,1152]{1,0:T(8,128)(2,1)} %txt.1, f32[1]{0:T(128)S(6)} %copy.11.scale_ref, f32[1]{0:T(128)S(6)} %copy.12.bias_ref), custom_call_target="tpu_custom_call" | custom-call | tf_op jit(solution)/shard_map/pallas_call | solution.py:163
  73.9 0.6 slice.3
  74.5 1.4 %copy.9 = f32[512,1152]{1,0:T(8,128)} copy(f32[512,1152]{1,0:T(8,128)S(1)} %get-tuple-element.10) | data formatting | bytes 4718592
  75.9 1.4 %copy.10 = f32[512,1152]{1,0:T(8,128)} copy(f32[512,1152]{1,0:T(8,128)S(1)} %get-tuple-element.11) | data formatting | bytes 4718592
Async XLA Ops:
  1.9 1.3 %copy-start = (bf16[512,1152]{1,0:T(8,128)(2,1)S(1)}, bf16[512,1152]{1,0:T(8,128)(2,1)}, u32[]{:S(2)}) copy-start(bf16[512,1152]{1,0:T(8,128)(2,1)} %img.1) | copy-start | bytes 3538948

commit v2 on v0

v2 whole, which is shorter than its diff:
```python
import functools

import jax
import jax.numpy as jnp
from jax import lax
from jax.experimental import pallas as pl
from jax.experimental.pallas import tpu as pltpu
from jax.sharding import PartitionSpec as P

MESH = pl.DeviceIdType.MESH
WINDOW = 5
EPS = 1e-06
TEXT, IMAGE = 0, 1
SHARED, RELAYED, DIRECT, SIBLING = range(4)
HELD = 256
MIB = 1024 * 1024


def pieces_of(rows):
    cuts = [(TEXT, 0, 256), (TEXT, 256, 256), (IMAGE, 0, 256), (IMAGE, 256, 128), (IMAGE, 384, 64), (IMAGE, 448, 64)]
    assert rows == 512
    return cuts


def inverse_length(rows):
    return lax.rsqrt(jnp.sum(rows * rows, axis=1, keepdims=True) + EPS)


def cosines(held, other):
    return lax.dot_general(held, other, (((1,), (1,)), ((), ())), preferred_element_type=jnp.float32)


def unit_gradient(summed, raw, factor):
    unit = raw.astype(jnp.float32) * factor
    along = jnp.sum(summed * unit, axis=1, keepdims=True)
    return (summed - unit * along) * factor


def exchange(n, img, txt, scale_ref, bias_ref,
             image_grad, text_total, text_unit, text_raw, text_factor, last, row_loss, params,
             image_total, image_unit, image_raw, image_factor, buf, chunk, loss_acc,
             load_sem, send_sem, recv_sem):
    rows = img.shape[0]
    pieces = pieces_of(rows)
    me = lax.axis_index("dp")
    core = lax.rem(me, 2)
    sibling = me + 1 - 2 * core
    step = 2 * core - 1
    ahead = lax.rem(me + 2 * step + n, n)
    behind = lax.rem(me - 2 * step + n, n)
    across = lax.rem(me + step + n, n)

    barrier = pltpu.get_barrier_semaphore()
    for other in (behind, across, sibling):
        pl.semaphore_signal(barrier, inc=1, device_id=(other,), device_id_type=MESH)
    loads = [
        pltpu.make_async_copy(source, target, load_sem.at[i])
        for i, (source, target) in enumerate(
            ((txt, text_raw), (img, image_raw))
        )
    ]
    for load in loads:
        load.start()
    pl.semaphore_wait(barrier, 3)

    def remote(source, way, piece, target):
        kind, first, size = pieces[piece]
        return pltpu.make_async_remote_copy(
            source, buf.at[way, kind, pl.ds(first, size)], send_sem.at[way, piece], recv_sem.at[way, piece],
            device_id=(target,), device_id_type=MESH,
        )

    def own_rows(piece):
        kind, first, size = pieces[piece]
        return (txt, img)[kind].at[pl.ds(first, size)]

    def landed(way, piece):
        kind, first, size = pieces[piece]
        return buf.at[way, kind, pl.ds(first, size)]

    everything = range(len(pieces))
    shared = [remote(own_rows(p), SHARED, p, ahead) for p in everything]
    direct = [remote(landed(SIBLING, p), DIRECT, p, across) for p in everything]
    beside = [remote(own_rows(p), SIBLING, p, sibling) for p in everything]
    relays = [remote(landed(SHARED, p), RELAYED, p, sibling) for p in everything]
    for copy in shared:
        copy.start()
    for copy in beside:
        copy.start()

    for load in loads:
        load.wait()
    scale = scale_ref[0]
    bias = bias_ref[0]
    params[0:8] = jnp.full((8, 128), scale, jnp.float32)
    params[8:16] = jnp.full((8, 128), bias, jnp.float32)

    for raw, unit, factor_ref in ((text_raw, text_unit, text_factor), (image_raw, image_unit, image_factor)):
        @pl.loop(0, rows // 128)
        def _(tile):
            span = pl.ds(pl.multiple_of(tile * 128, 128), 128)
            values = raw[span].astype(jnp.float32)
            factor = inverse_length(values)
            factor_ref[span] = factor
            unit[span] = (values * factor).astype(jnp.bfloat16)

    image_total[...] = jnp.zeros_like(image_total)
    text_total[...] = jnp.zeros_like(text_total)
    loss_acc[...] = jnp.zeros_like(loss_acc)

    def pairs(kind, other, size, offset=None):
        held_unit, total = ((image_unit, image_total), (text_unit, text_total))[kind]
        for tile in range(rows // HELD):
            held = pl.ds(tile * HELD, HELD)
            logits = scale * cosines(held_unit[held], other[...]) + bias
            grown = jnp.exp(logits)
            above = 1.0 + grown
            share = grown * pl.reciprocal(above)
            if offset is not None:
                row = lax.broadcasted_iota(jnp.int32, logits.shape, 0) + tile * HELD
                column = lax.broadcasted_iota(jnp.int32, logits.shape, 1)
                positive = row - column == offset
                share = share - jnp.where(positive, 1.0, 0.0)
            if kind == TEXT:
                small = grown * (1.0 - grown * (0.5 - grown * (1.0 / 3.0)))
                loss = jnp.where(grown < 0.0078125, small, jnp.log(above))
                if offset is not None:
                    loss = loss - jnp.where(positive, logits, 0.0)
                loss_acc[held] += functools.reduce(jnp.add, [loss[:, i:i + 128] for i in range(0, size, 128)])
            weights = (scale * share).astype(jnp.bfloat16)
            total[held] += jnp.dot(weights, other[...], preferred_element_type=jnp.float32)

    def unit_rows(source, target, size):
        step = min(size, 128)
        for first in range(0, size, step):
            values = source[first:first + step].astype(jnp.float32)
            target[first:first + step] = (values * inverse_length(values)).astype(jnp.bfloat16)

    def received(way, kind, first, size):
        unit_rows(buf.at[way, kind, pl.ds(first, size)], chunk, size)
        pairs(kind, chunk.at[pl.ds(0, size)], size)

    for kind, unit in ((TEXT, text_unit), (IMAGE, image_unit)):
        @pl.loop(0, rows // 256)
        def _(tile):
            first = pl.multiple_of(tile * 256, 256)
            pairs(kind, unit.at[pl.ds(first, 256)], 256, first)

    for copy in beside:
        copy.wait_recv()
    for kind in (TEXT, IMAGE):
        @pl.loop(0, rows // 256)
        def _(tile):
            received(SIBLING, kind, pl.multiple_of(tile * 256, 256), 256)

    for copy in direct:
        copy.start()

    def finish_images():
        @pl.loop(0, rows // 64)
        def _(tile):
            span = pl.ds(pl.multiple_of(tile * 64, 64), 64)
            image_grad[span] = unit_gradient(image_total[span], image_raw[span], image_factor[span])

        summed = lax.dot_general(
            jnp.full((8, 128), 1.0, jnp.float32), loss_acc[...], (((1,), (1,)), ((), ())),
            preferred_element_type=jnp.float32, precision=lax.Precision.HIGHEST,
        )
        row_loss[...] = summed[0:1] * (1.0 / (WINDOW * rows))

    def near(piece):
        shared[piece].wait_recv()
        relays[piece].start()
        received(SHARED, *pieces[piece])
        relays[piece].wait_recv()
        received(RELAYED, *pieces[piece])

    def far(piece):
        direct[piece].wait_recv()
        received(DIRECT, *pieces[piece])

    texts = [p for p in everything if pieces[p][0] == TEXT]
    images = [p for p in everything if pieces[p][0] == IMAGE]
    for piece in everything:
        near(piece)
    for piece in texts:
        far(piece)
    finish_images()
    for piece in images[:-1]:
        far(piece)
    direct[images[-1]].wait_recv()
    unit_rows(landed(DIRECT, images[-1]), last, last.shape[0])
    for copy in shared + direct + beside + relays:
        copy.wait_send()


def complete(image_done, text_total, text_unit, text_raw, text_factor, last, loss_done, params,
             row_loss, image_grad, text_grad, out, sem):
    rows = text_unit.shape[0]
    size = last.shape[0]
    tile = 128
    copies = [pltpu.make_async_copy(image_done, image_grad, sem.at[0]), pltpu.make_async_copy(loss_done, row_loss, sem.at[1])]
    for copy in copies:
        copy.start()
    scale = params[0:1, 0:size]
    bias = params[8:9, 0:size]
    for i in range(rows // tile):
        held = pl.ds(i * tile, tile)
        grown = jnp.exp(scale * cosines(text_unit[held], last[...]) + bias)
        weights = (scale * (grown * pl.reciprocal(1.0 + grown))).astype(jnp.bfloat16)
        summed = text_total[held] + jnp.dot(weights, last[...], preferred_element_type=jnp.float32)
        out[held] = unit_gradient(summed, text_raw[held], text_factor[held])
        copy = pltpu.make_async_copy(out.at[held], text_grad.at[held], sem.at[2 + i])
        copy.start()
        copies.append(copy)
    for copy in copies:
        copy.wait()


def local(n, image_embed, text_embed, logit_scale, logit_bias):
    rows, width = image_embed.shape
    pieces = pieces_of(rows)
    f32, bf16 = jnp.float32, jnp.bfloat16
    anywhere = pl.BlockSpec(memory_space=pl.ANY)
    hbm = pl.BlockSpec(memory_space=pltpu.HBM)
    vmem = pl.BlockSpec(memory_space=pltpu.VMEM)
    smem = pl.BlockSpec(memory_space=pltpu.SMEM)
    last_rows = pieces[-1][2]
    between = pl.pallas_call(
        functools.partial(exchange, n),
        out_shape=(
            pltpu.VMEM((rows, width), f32),
            pltpu.VMEM((rows, width), f32),
            pltpu.VMEM((rows, width), bf16),
            pltpu.VMEM((rows, width), bf16),
            pltpu.VMEM((rows, 1), f32),
            pltpu.VMEM((last_rows, width), bf16),
            pltpu.VMEM((1, rows), f32),
            pltpu.VMEM((16, 128), f32),
        ),
        in_specs=[hbm, hbm, smem, smem],
        out_specs=[vmem] * 8,
        scratch_shapes=[
            pltpu.VMEM((rows, width), f32),
            pltpu.VMEM((rows, width), bf16),
            pltpu.VMEM((rows, width), bf16),
            pltpu.VMEM((rows, 1), f32),
            pltpu.VMEM((4, 2, rows, width), bf16),
            pltpu.VMEM((256, width), bf16),
            pltpu.VMEM((rows, 128), f32),
            pltpu.SemaphoreType.DMA((2,)),
            pltpu.SemaphoreType.DMA((4, len(pieces))),
            pltpu.SemaphoreType.DMA((4, len(pieces))),
        ],
        compiler_params=pltpu.CompilerParams(collective_id=0, has_side_effects=True, vmem_limit_bytes=55 * MIB),
    )(image_embed, text_embed, logit_scale, logit_bias)
    row_loss, image_grad, text_grad = pl.pallas_call(
        complete,
        out_shape=(
            jax.ShapeDtypeStruct((1, rows), f32),
            jax.ShapeDtypeStruct((rows, width), f32),
            jax.ShapeDtypeStruct((rows, width), f32),
        ),
        in_specs=[vmem] * 8,
        out_specs=[anywhere] * 3,
        scratch_shapes=[pltpu.VMEM((rows, width), f32), pltpu.SemaphoreType.DMA((2 + rows // 128,))],
        compiler_params=pltpu.CompilerParams(vmem_limit_bytes=40 * MIB),
    )(*between)
    return row_loss[0], image_grad, text_grad


def solution(mesh):
    return jax.shard_map(
        functools.partial(local, mesh.shape["dp"]),
        mesh=mesh,
        in_specs=(P("dp", None), P("dp", None), P(), P()),
        out_specs=(P("dp"), P("dp", None), P("dp", None)),
        check_vma=False,
    )
```

time: 147 us -> 66.4 us (0.45); the launches traced: 145 us -> 66.3 us
  waiting for transfers between devices: 100 us -> 0 us
  Pallas kernels: 0 us -> 64.2 us
  matrix products: 17.8 us -> 0 us
  starting transfers between devices: 16.5 us -> 0 us
  other arithmetic: 8.36 us -> 0 us
    ppermute x8 -> x0, waiting for transfers between devices: 100 us -> none  [shifted(): return lax.ppermute(block, axis, route)]
    pallas_call x0 -> x2, Pallas kernels: none -> 64.2 us  [the longest x1 61.7 us: local(): pl.pallas_call(functools.partial(exchange, n), out_shape=(pltpu.VMEM((row...]
    dot_general x15 -> x0, matrix products: 17.8 us -> none  [the longest x5 7.34 us: pair_block(): lax.dot_general(image_rows, text_rows, (((1,), (1,)), ((), ())), preferre...]
    ppermute x8 -> x0, starting transfers between devices: 16.5 us -> none  [shifted(): return lax.ppermute(block, axis, route)]
    div x3 -> x0, other arithmetic: 4.36 us -> none  [the longest x2 3.78 us: unit_grad(): return (grad_unit - unit_values * along_unit) / length]
    reduce_sum x2 -> x0, other arithmetic: 1.98 us -> none  [unit_rows(): jnp.sum(values * values, axis=1, keepdims=True) + eps_norm]
    broadcast_in_dim x1 -> x0, other arithmetic: 1.63 us -> none  [local(): payload = text_rows[None]]
  transfers between devices with their start and end apart: 8 -> 0, of which waited for: 5 -> 0; matrix products, arithmetic and copies ran while one was open for 13% -> 0% of each run, Pallas kernels for 0% -> 0%
where the time goes in v2:
time: 66.4 us; the launch traced here: 66.3 us
  Pallas kernels  64.2 us (97%)
  between operations  2.11 us (3%)
    pallas_call x1, Pallas kernels, local(): pl.pallas_call(functools.partial(exchange, n), out_shape=(pltpu.VMEM((row...  61.7 us
    pallas_call x1, Pallas kernels, local(): pl.pallas_call(complete, out_shape=(jax.ShapeDtypeStruct((1, rows), f32),...  2.48 us

profile of v2, /device:TPU:0, one launch (start us, length us, event | category | flops | bytes accessed | tf_op | source)
XLA Modules:
  0.0 66.3 jit_solution(15731298005455846209)
XLA Ops:
  1.9 61.7 %shard_map.67 = (f32[512,1152]{1,0:T(8,128)S(1)}, f32[512,1152]{1,0:T(8,128)S(1)}, bf16[512,1152]{1,0:T(8,128)(2,1)S(1)}, bf16[512,1152]{1,0:T(8,128)(2,1)S(1)},...) custom-call(bf16[512,1152]{1,0:T(8,128)(2,1)} %img.1, ...), custom_call_target="tpu_custom_call" | custom-call | tf_op jit(solution)/shard_map/pallas_call | solution.py:229
  63.6 2.5 %shard_map.68 = (f32[1,512]{1,0:T(1,128)}, f32[512,1152]{1,0:T(8,128)}, f32[512,1152]{1,0:T(8,128)}) custom-call(f32[512,1152]{1,0:T(8,128)S(1)} %get-tuple-element.14.image_done, f32[512,1152]{1,0:T(8,128)S(1)} %get-tuple-element.15.text_total, bf16[512,1152]{1,0:T(8,128)(2,1)S(1)} %get-tuple-element.16.text_unit, ...), custom_call_target="tpu_custom_call" | custom-call | tf_op jit(solution)/shard_map/pallas_call | solution.py:257

commit v3 on v2

--- a/solution.py
+++ b/solution.py
@@ -148,13 +148,13 @@
 
     for copy in beside:
         copy.wait_recv()
+    for copy in direct:
+        copy.start()
+
     for kind in (TEXT, IMAGE):
         @pl.loop(0, rows // 256)
         def _(tile):
             received(SIBLING, kind, pl.multiple_of(tile * 256, 256), 256)
-
-    for copy in direct:
-        copy.start()
 
     def finish_images():
         @pl.loop(0, rows // 64)

time: 66.4 us -> 66.4 us (level)
  no operation moved by 1% of the time
where the time goes in v3:
time: 66.4 us; the launch traced here: 66.3 us
  Pallas kernels  64.2 us (97%)
  between operations  2.11 us (3%)
    pallas_call x1, Pallas kernels, local(): pl.pallas_call(functools.partial(exchange, n), out_shape=(pltpu.VMEM((row...  61.7 us
    pallas_call x1, Pallas kernels, local(): pl.pallas_call(complete, out_shape=(jax.ShapeDtypeStruct((1, rows), f32),...  2.48 us

profile of v3, /device:TPU:0, one launch (start us, length us, event | category | flops | bytes accessed | tf_op | source)
XLA Modules:
  0.0 66.3 jit_solution(439906880486190074)
XLA Ops:
  1.9 61.7 %shard_map.67 = (f32[512,1152]{1,0:T(8,128)S(1)}, f32[512,1152]{1,0:T(8,128)S(1)}, bf16[512,1152]{1,0:T(8,128)(2,1)S(1)}, bf16[512,1152]{1,0:T(8,128)(2,1)S(1)},...) custom-call(bf16[512,1152]{1,0:T(8,128)(2,1)} %img.1, ...), custom_call_target="tpu_custom_call" | custom-call | tf_op jit(solution)/shard_map/pallas_call | solution.py:229
  63.6 2.5 %shard_map.68 = (f32[1,512]{1,0:T(1,128)}, f32[512,1152]{1,0:T(8,128)}, f32[512,1152]{1,0:T(8,128)}) custom-call(f32[512,1152]{1,0:T(8,128)S(1)} %get-tuple-element.14.image_done, f32[512,1152]{1,0:T(8,128)S(1)} %get-tuple-element.15.text_total, bf16[512,1152]{1,0:T(8,128)(2,1)S(1)} %get-tuple-element.16.text_unit, ...), custom_call_target="tpu_custom_call" | custom-call | tf_op jit(solution)/shard_map/pallas_call | solution.py:257

commit v4 on v3

--- a/solution.py
+++ b/solution.py
@@ -17,7 +17,7 @@
 
 
 def pieces_of(rows):
-    cuts = [(TEXT, 0, 256), (TEXT, 256, 256), (IMAGE, 0, 256), (IMAGE, 256, 128), (IMAGE, 384, 64), (IMAGE, 448, 64)]
+    cuts = [(TEXT, 0, 256), (TEXT, 256, 256), (IMAGE, 0, 256), (IMAGE, 256, 192), (IMAGE, 448, 64)]
     assert rows == 512
     return cuts
 
@@ -51,7 +51,7 @@
     across = lax.rem(me + step + n, n)
 
     barrier = pltpu.get_barrier_semaphore()
-    for other in (behind, across, sibling):
+    for other in (across, behind, sibling):
         pl.semaphore_signal(barrier, inc=1, device_id=(other,), device_id_type=MESH)
     loads = [
         pltpu.make_async_copy(source, target, load_sem.at[i])
@@ -131,7 +131,7 @@
             total[held] += jnp.dot(weights, other[...], preferred_element_type=jnp.float32)
 
     def unit_rows(source, target, size):
-        step = min(size, 128)
+        step = 128 if size % 128 == 0 else 64
         for first in range(0, size, step):
             values = source[first:first + step].astype(jnp.float32)
             target[first:first + step] = (values * inverse_length(values)).astype(jnp.bfloat16)

time: 66.4 us -> 66.3 us (level)
  no operation moved by 1% of the time
where the time goes in v4:
time: 66.3 us; the launch traced here: 66.2 us
  Pallas kernels  64.1 us (97%)
  between operations  2.11 us (3%)
    pallas_call x1, Pallas kernels, local(): pl.pallas_call(functools.partial(exchange, n), out_shape=(pltpu.VMEM((row...  61.6 us
    pallas_call x1, Pallas kernels, local(): pl.pallas_call(complete, out_shape=(jax.ShapeDtypeStruct((1, rows), f32),...  2.48 us

profile of v4, /device:TPU:0, one launch (start us, length us, event | category | flops | bytes accessed | tf_op | source)
XLA Modules:
  0.0 66.2 jit_solution(6542090711414488640)
XLA Ops:
  1.9 61.6 %shard_map.67 = (f32[512,1152]{1,0:T(8,128)S(1)}, f32[512,1152]{1,0:T(8,128)S(1)}, bf16[512,1152]{1,0:T(8,128)(2,1)S(1)}, bf16[512,1152]{1,0:T(8,128)(2,1)S(1)},...) custom-call(bf16[512,1152]{1,0:T(8,128)(2,1)} %img.1, ...), custom_call_target="tpu_custom_call" | custom-call | tf_op jit(solution)/shard_map/pallas_call | solution.py:229
  63.5 2.5 %shard_map.68 = (f32[1,512]{1,0:T(1,128)}, f32[512,1152]{1,0:T(8,128)}, f32[512,1152]{1,0:T(8,128)}) custom-call(f32[512,1152]{1,0:T(8,128)S(1)} %get-tuple-element.14.image_done, f32[512,1152]{1,0:T(8,128)S(1)} %get-tuple-element.15.text_total, bf16[512,1152]{1,0:T(8,128)(2,1)S(1)} %get-tuple-element.16.text_unit, ...), custom_call_target="tpu_custom_call" | custom-call | tf_op jit(solution)/shard_map/pallas_call | solution.py:257
